TPU v7x, 512 devices: a whole 4x8x8 slice. The times are simulated.
512 devices in a mesh: frame: 8 (over y), head: 32 (over x, z), rep: 2 (over core).
Axes of the slice: x: 4, y: 8, z: 8, core: 2. Of those that a mesh axis runs over, the one named last changes fastest.
Arguments:
- queries: bfloat16 [32768, 4096], P(('rep', 'frame', 'head')), parts along dimension 0, may hold values from -64 to 64
- key_rows: bfloat16 [32768, 4096], P(('rep', 'frame', 'head')), parts along dimension 0, may hold values from -64 to 64
- values: bfloat16 [32768, 4096], P(('rep', 'frame', 'head')), parts along dimension 0, may hold values from -6 to 6
- slot_frame: int32 [32], replicated, may hold values from 0 to 31, as said below
- radial_tiles: int32 [160, 3], replicated, may hold values from 0 to 512, as said below
Outputs:
- attended: bfloat16 [32768, 4096], P(('rep', 'frame', 'head')), parts along dimension 0
There are 2 independent parts, one for each index of `rep`. A program takes and returns all parts, laid end to end along the dimension named above; an argument that names none is the same for every part. Nothing has to cross between parts.
Inputs may be any that keep to these rules, and one draw needn't show every extreme that they name: Slot s (rows s * 512 to (s + 1) * 512 - 1) holds latent frame slot_frame[s]; every frame is held once, and slot_frame[s] // 4 == s // 4. `radial_tiles`: each row is (query frame, key frame, half-width). Half-width 0 marks an empty row. Every frame has a row pairing it with itself with half-width 512 // 2 or more; no pair of frames has two nonempty rows; the frames of a nonempty row may lie anywhere in the sequence.
All inputs are finite; a program needn't handle non-finite values.
Results may differ from a plain program's by a relative error of at most 0.008.
Values may be sent and summed in bfloat16 or wider, within the bound.
A program may use at most 128 MiB of HBM per device.

v0:
```python
import math

import jax
import jax.numpy as jnp
from jax import lax
from jax.sharding import PartitionSpec as P

HEADS = 32
HEAD_DIM = 128
FRAME_PIX = 512


def update(
    carry_state, own_index, query_frame, keys_block, vals_block, key_pos, row_width, score_scale
):
    row_top, row_total, weighted = carry_state
    local_heads = query_frame.shape[1]
    piece_rows = keys_block.shape[0]
    key_heads = keys_block.reshape(piece_rows, local_heads, HEAD_DIM)
    val_heads = vals_block.reshape(piece_rows, local_heads, HEAD_DIM)
    positions = jnp.arange(query_frame.shape[0], dtype=jnp.int32)
    scores = (
        jnp.einsum("phe,khe->phk", query_frame, key_heads, preferred_element_type=jnp.float32)
        * score_scale
    )
    allowed = (jnp.abs(positions[:, None] - key_pos[None, :]) < row_width[None, :])[:, None, :]
    masked = jnp.where(allowed, scores, -1e30)
    old_top = row_top[own_index]
    new_top = jnp.maximum(old_top, jnp.max(masked, axis=-1))
    weight = jnp.where(allowed, jnp.exp(masked - new_top[..., None]), 0.0)
    shrink = jnp.exp(old_top - new_top)
    new_total = row_total[own_index] * shrink + jnp.sum(weight, axis=-1)
    product = jnp.einsum(
        "phk,khe->phe", weight.astype(jnp.bfloat16), val_heads, preferred_element_type=jnp.float32
    )
    new_weighted = weighted[own_index] * shrink[..., None] + product
    return (
        row_top.at[own_index].set(new_top),
        row_total.at[own_index].set(new_total),
        weighted.at[own_index].set(new_weighted),
    )


def on_device(queries, key_rows, values, slot_frame, radial_tiles):
    head_devices = lax.axis_size("head")
    local_heads = HEADS // head_devices
    score_scale = 1.0 / math.sqrt(HEAD_DIM)
    q_local, k_local, v_local = (
        lax.all_to_all(queries, "head", split_axis=1, concat_axis=0, tiled=True),
        lax.all_to_all(key_rows, "head", split_axis=1, concat_axis=0, tiled=True),
        lax.all_to_all(values, "head", split_axis=1, concat_axis=0, tiled=True),
    )
    frame_rows = q_local.shape[0]
    own_frames = frame_rows // FRAME_PIX
    frame_count = slot_frame.shape[0]
    query_frames = q_local.reshape(own_frames, FRAME_PIX, local_heads, HEAD_DIM)
    frame_ids = jnp.arange(frame_count, dtype=jnp.int32)
    on_query = (radial_tiles[:, 0:1] == frame_ids[None, :]).astype(jnp.int32)
    on_key = (radial_tiles[:, 1:2] == frame_ids[None, :]).astype(jnp.int32)
    table = jnp.dot((on_query * radial_tiles[:, 2:3]).T, on_key)
    holder = (slot_frame[:, None] == frame_ids[None, :]).astype(jnp.int32)
    slot_width = jnp.dot(jnp.dot(holder, table), holder.T)
    frame_index = lax.axis_index("frame")
    my_width = lax.dynamic_slice_in_dim(slot_width, frame_index * own_frames, own_frames, 0)
    key_positions = jnp.arange(FRAME_PIX, dtype=jnp.int32)
    start_state = (
        jnp.full((own_frames, FRAME_PIX, local_heads), -1e30, jnp.float32),
        jnp.zeros((own_frames, FRAME_PIX, local_heads), jnp.float32),
        jnp.zeros((own_frames, FRAME_PIX, local_heads, HEAD_DIM), jnp.float32),
    )
    keys_piece = lax.all_gather(k_local, "frame", axis=0, tiled=True)
    vals_piece = lax.all_gather(v_local, "frame", axis=0, tiled=True)
    piece_rows = keys_piece.shape[0]

    def per_frame(frame_step, carried_state):
        inside = (frame_step >= 0) & (frame_step < frame_count)
        safe_slot = jnp.clip(frame_step, 0, frame_count - 1)
        keys_frame = lax.dynamic_slice_in_dim(keys_piece, frame_step * FRAME_PIX, FRAME_PIX, 0)
        vals_frame = lax.dynamic_slice_in_dim(vals_piece, frame_step * FRAME_PIX, FRAME_PIX, 0)
        for own_index in range(own_frames):
            tile_width = jnp.where(inside, my_width[own_index, safe_slot], 0)
            row_width = jnp.full((FRAME_PIX,), tile_width, jnp.int32)

            def attend(
                carried,
                own_index=own_index,
                row_width=row_width,
                keys_frame=keys_frame,
                vals_frame=vals_frame,
            ):
                return update(
                    carried,
                    own_index,
                    query_frames[own_index],
                    keys_frame,
                    vals_frame,
                    key_positions,
                    row_width,
                    score_scale,
                )

            def keep(carried):
                return carried

            carried_state = lax.cond(tile_width > 0, attend, keep, carried_state)
        return carried_state

    final = lax.fori_loop(0, piece_rows // FRAME_PIX, per_frame, start_state)
    outcome = (final[2] / final[1][..., None]).astype(jnp.bfloat16)
    outcome = outcome.reshape(frame_rows, local_heads * HEAD_DIM)
    return lax.all_to_all(outcome, "head", split_axis=0, concat_axis=1, tiled=True)


def solution(mesh):
    placed = (
        P(("rep", "frame", "head"), None),
        P(("rep", "frame", "head"), None),
        P(("rep", "frame", "head"), None),
        P(),
        P(),
    )
    return jax.shard_map(
        on_device,
        mesh=mesh,
        in_specs=placed,
        out_specs=P(("rep", "frame", "head"), None),
        check_vma=False,
    )
```

profile of v0, /device:TPU:64, one launch (start us, length us, event | category | flops | bytes accessed | tf_op | source)
XLA Modules:
  0.0 338.9 jit_solution(15636173450621921823)
XLA Ops:
  6.6 1.0 copy-done
  7.7 30.1 %all_to_all.73 = bf16[64,32,128]{2,0,1:T(8,128)(2,1)} all-to-all(bf16[64,32,128]{2,0,1:T(8,128)(2,1)S(1)} %copy_bitcast_fusion.3), channel_id=1, replica_groups=mesh['frame'=8,'head'=32,'rep'=2] {'head'}, dimensions={1} | all-to-all | bytes 1048576 | tf_op jit(solution)/shard_map/all_to_all | solution.py:50
  37.9 1.2 copy_bitcast_fusion.2
  39.1 21.7 %all_to_all.74 = bf16[64,32,128]{2,0,1:T(8,128)(2,1)} all-to-all(bf16[64,32,128]{2,0,1:T(8,128)(2,1)S(1)} %copy_bitcast_fusion.2), channel_id=1, replica_groups=mesh['frame'=8,'head'=32,'rep'=2] {'head'}, dimensions={1} | all-to-all | bytes 1048576 | tf_op jit(solution)/shard_map/all_to_all | solution.py:51
  61.8 4.9 %all-to-all-start.2 = ((bf16[64,32,128]{2,0,1:T(8,128)(2,1)}), bf16[64,32,128]{2,0,1:T(8,128)(2,1)S(1)}, u32[]{:S(2)}, u32[]{:S(2)}) async-start(bf16[64,32,128]{2,0,1:T(8,128)(2,1)} %copy_bitcast_fusion.1), calls=%async_computation.2 | async-start | bytes 1048576 | tf_op jit(solution)/shard_map/all_to_all | solution.py:49
  67.3 16.1 %all-to-all-done.2 = bf16[64,32,128]{2,0,1:T(8,128)(2,1)S(1)} async-done(((bf16[64,32,128]{2,0,1:T(8,128)(2,1)}), bf16[64,32,128]{2,0,1:T(8,128)(2,1)S(1)}, u32[]{:S(2)}, u32[]{:S(2)}) %all-to-all-start.2) | async-done | bytes 524320 | tf_op jit(solution)/shard_map/all_to_all | solution.py:49
  83.4 7.9 %all-gather.3.cloned.1.call-done = bf16[16384,128]{1,0:T(8,128)(2,1)} async-done(((bf16[2048,128]{1,0:T(8,128)(2,1)}), bf16[16384,128]{1,0:T(8,128)(2,1)}) %all-gather.3.cloned.1.call-update) | async-done | bytes 4194320 | tf_op jit(solution)/shard_map/all_gather | solution.py:71
  91.3 58.3 %all-gather.5.cloned.1.call-done = bf16[16384,128]{1,0:T(8,128)(2,1)} async-done(((bf16[2048,128]{1,0:T(8,128)(2,1)}), bf16[16384,128]{1,0:T(8,128)(2,1)}) %all-gather.5.cloned.1.call-update) | async-done | bytes 4194320 | tf_op jit(solution)/shard_map/all_gather | solution.py:72
  149.7 153.4 %while.31 = (s32[]{:T(128)}, f32[4,512,1]{1,2,0:T(1,128)S(1)}, f32[4,512,1]{1,2,0:T(1,128)S(1)}, f32[4,512,1,128]{3,1,2,0:T(8,128)S(1)}, s32[4,32]{1,0:T(4,128)S...) while((s32[]{:T(128)}, f32[4,512,1]{1,2,0:T(1,128)S(1)}, ...), condition=%wide.region_17.18_spmd.clone.clone, body=%wide.region_0.17_spmd.clone.clone.sunk | while | flops 556277760 | bytes 19041072 | solution.py:108
  152.8 1.0 constant_dynamic-slice_fusion.10
  153.8 1.6 conditional.16
  158.5 1.0 constant_dynamic-slice_fusion.10
  159.5 1.6 conditional.17
  164.3 1.0 constant_dynamic-slice_fusion.10
  165.3 1.6 conditional.18
  170.0 1.0 constant_dynamic-slice_fusion.10
  171.0 1.6 conditional.16
  172.6 1.6 conditional.17
  174.3 1.6 conditional.19
  178.9 1.0 constant_dynamic-slice_fusion.10
  183.1 1.0 constant_dynamic-slice_fusion.10
  187.2 1.0 constant_dynamic-slice_fusion.10
  191.4 1.0 constant_dynamic-slice_fusion.10
  195.5 1.0 constant_dynamic-slice_fusion.10
  196.5 1.6 conditional.17
  198.2 1.6 conditional.19
  202.8 1.0 constant_dynamic-slice_fusion.10
  203.8 1.6 conditional.16
  208.6 1.0 constant_dynamic-slice_fusion.10
  212.7 1.0 constant_dynamic-slice_fusion.10
  216.9 1.0 constant_dynamic-slice_fusion.10
  217.9 1.6 conditional.18
  226.8 1.0 constant_dynamic-slice_fusion.10
  230.9 1.0 constant_dynamic-slice_fusion.10
  235.1 1.0 constant_dynamic-slice_fusion.10
  239.2 1.0 constant_dynamic-slice_fusion.10
  243.3 1.0 constant_dynamic-slice_fusion.10
  247.5 1.0 constant_dynamic-slice_fusion.10
  251.6 1.0 constant_dynamic-slice_fusion.10
  252.7 1.6 conditional.17
  257.4 1.0 constant_dynamic-slice_fusion.10
  261.5 1.0 constant_dynamic-slice_fusion.10
  265.7 1.0 constant_dynamic-slice_fusion.10
  266.7 1.6 conditional.19
  271.4 1.0 constant_dynamic-slice_fusion.10
  275.6 1.0 constant_dynamic-slice_fusion.10
  289.0 1.6 conditional.16
  303.5 27.7 %all_to_all.75 = bf16[32,64,128]{2,1,0:T(8,128)(2,1)S(1)} all-to-all(bf16[32,64,128]{2,1,0:T(8,128)(2,1)S(1)} %bitcast.208), channel_id=1, replica_groups=mesh['frame'=8,'head'=32,'rep'=2] {'head'}, dimensions={0} | all-to-all | bytes 1048576 | tf_op jit(solution)/shard_map/all_to_all | solution.py:111
  (300 shorter events, 51.7 us)
Async XLA Ops:
  6.5 1.0 copy-start
  6.5 54.3 %copy-start.1 = (bf16[64,4096]{1,0:T(8,128)(2,1)S(1)}, bf16[64,4096]{1,0:T(8,128)(2,1)}, u32[]{:S(2)}) copy-start(bf16[64,4096]{1,0:T(8,128)(2,1)} %param.39) | copy-start | bytes 1572868
  6.5 60.1 %copy-start.2 = (s32[160,3]{0,1:T(4,128)S(1)}, s32[160,3]{0,1:T(4,128)}, u32[]{:S(2)}) copy-start(s32[160,3]{0,1:T(4,128)} %param.43) | copy-start | bytes 5764
  6.5 60.5 %copy-start.3 = (s32[32]{0:T(128)S(1)}, s32[32]{0:T(128)}, u32[]{:S(2)}) copy-start(s32[32]{0:T(128)} %param.42) | copy-start | bytes 388
  6.5 84.8 %all-gather.3.cloned.1.call-start = ((), (), s32[]{:S(2)}) async-start(), calls=%async_computation.4 | async-start | bytes 4718592 | tf_op jit(solution)/shard_map/all_gather | solution.py:71
  37.8 111.8 %all-gather.5.cloned.1.call-start = ((), (), s32[]{:S(2)}) async-start(), calls=%async_computation.5 | async-start | bytes 4718592 | tf_op jit(solution)/shard_map/all_gather | solution.py:72
  61.8 21.7 %all-to-all-start.2 = ((bf16[64,32,128]{2,0,1:T(8,128)(2,1)}), bf16[64,32,128]{2,0,1:T(8,128)(2,1)S(1)}, u32[]{:S(2)}, u32[]{:S(2)}) async-start(bf16[64,32,128]{2,0,1:T(8,128)(2,1)} %copy_bitcast_fusion.1), calls=%async_computation.2 | async-start | bytes 1048576 | tf_op jit(solution)/shard_map/all_to_all | solution.py:49
Sparse Core Ops, SparseCore 0:
  38.0 53.3 all-gather.2
  93.4 56.1 all-gather.4
where the time goes:
time: 341 us; the launch traced here: 339 us
  waiting for transfers between devices  82.3 us (24%)
  loops' own time  82.1 us (24%)
  blocking collectives  79.6 us (23%)
  local copies, waits for them, and re-layouts  55.4 us (16%)
  matrix products  14.9 us (4%)
  between operations  13.5 us (4%)
  other arithmetic  6.19 us (2%)
  starting transfers between devices  4.94 us (1%)
    another operation x1, loops' own time, on_device(): final = lax.fori_loop(0, piece_rows // FRAME_PIX, per_frame, start_state)  79.4 us
    all_gather x1, waiting for transfers between devices, on_device(): vals_piece = lax.all_gather(v_local, 'frame', axis=0, tiled=True)  58.3 us
    dynamic_slice x32, local copies, waits for them, and re-layouts, per_frame(): lax.dynamic_slice_in_dim(vals_piece, frame_step * FRAME_PIX, FRAME_PIX, 0)  31.7 us
    all_to_all x1, blocking collectives, on_device(): lax.all_to_all(key_rows, 'head', split_axis=1, concat_axis=0, tiled=True)  30.1 us
    all_to_all x1, blocking collectives, on_device(): lax.all_to_all(outcome, 'head', split_axis=0, concat_axis=1, tiled=True)  27.7 us
    all_to_all x1, blocking collectives, on_device(): lax.all_to_all(values, 'head', split_axis=1, concat_axis=0, tiled=True)  21.7 us
    dynamic_slice x32, local copies, waits for them, and re-layouts, per_frame(): tile_width = jnp.where(inside, my_width[own_index, safe_slot], 0)  19.1 us
    all_to_all x1, waiting for transfers between devices, on_device(): lax.all_to_all(queries, 'head', split_axis=1, concat_axis=0, tiled=True)  16.1 us
  transfers between devices with their start and end apart: 3, of which 3 were waited for; matrix products, arithmetic and copies ran while one was open for 1% of the time, Pallas kernels for 0%

commit v1 on v0

v1 whole, which is shorter than its diff:
```python
import functools
import math

import jax
import jax.numpy as jnp
from jax import lax
from jax.experimental import pallas as pl
from jax.experimental.pallas import tpu as pltpu
from jax.sharding import PartitionSpec as P

HEADS = 32
HEAD_DIM = 128
FRAME_PIX = 512
GROUPS = 8
GROUP_FRAMES = 4
CHUNK = 64
SLOTS = 32
ROOMS = (12, 13, 14, 32)
MESH = pl.DeviceIdType.MESH
SCALE = math.log2(math.e) / math.sqrt(HEAD_DIM)


def place():
    y = lax.axis_index("frame")
    xz = lax.axis_index("head")
    x = lax.div(xz, 8)
    z = lax.rem(xz, 8)
    return y, x, lax.div(z, 2), lax.rem(z, 2), lax.axis_index("rep")


def partner(t, y, zh):
    return lax.rem(y + 3 * t, 8), lax.rem(zh + t + lax.div(t, 8), 4)


def send(src, dst, send_sem, recv_sem, here, there):
    same = (here[0] == there[0]) & (here[1] == there[1])

    @pl.when(same)
    def _():
        pltpu.make_async_copy(src, dst, recv_sem).start()

    @pl.when(jnp.logical_not(same))
    def _():
        pltpu.make_async_remote_copy(
            src_ref=src,
            dst_ref=dst,
            send_sem=send_sem,
            recv_sem=recv_sem,
            device_id=there,
            device_id_type=MESH,
        ).start()


def greet(there):
    pl.semaphore_signal(
        pltpu.get_barrier_semaphore(), inc=1, device_id=there, device_id_type=MESH
    )


def wait_bytes(ref, sem):
    pltpu.make_async_copy(ref, ref, sem).wait()


def chunk_of(y, x, zh, zl):
    turn = lax.rem(x + 16 - y - zh, 4)
    return lax.rem(2 * zh + jnp.where(zl == 1, turn + 1, 8 - turn), 8)


def gather_kernel(
    capacity,
    lists_ref,
    q_ref,
    k_ref,
    v_ref,
    q_out,
    k_out,
    v_out,
    k_spread,
    v_spread,
    k_other,
    v_other,
    k_stage,
    v_stage,
    k_relay,
    v_relay,
    send_sem,
    recv_sem,
    relay_sem,
    quarter_sem,
):
    y, x, zh, zl, core = place()
    z = 2 * zh + zl
    here = (y, x * 8 + z, core)
    right, left = lax.rem(x + 1, 4), lax.rem(x + 3, 4)

    def at(x2, zl2):
        return (y, x2 * 8 + 2 * zh + zl2, core)

    chunk = chunk_of(y, x, zh, zl)
    same_chunk = chunk == z
    same_query = lax.rem(y, 2) == zl

    def greet_senders(t, carry):
        y1, x1 = lax.rem(t, 8), lax.div(t, 8)

        @pl.when((y1 != y) | (x1 != x) | (chunk != z))
        def _():
            greet((y1, x1 * 8 + chunk, core))

        y2, z2 = 2 * lax.rem(t, 4) + zl, lax.div(t, 4)

        @pl.when((y2 != y) | (z2 != z))
        def _():
            greet((y2, x * 8 + z2, core))

        return carry

    lax.fori_loop(0, HEADS, greet_senders, 0)
    for mate in (at(right, zl), at(left, zl), at(x, 1 - zl)):
        greet(mate)
    pl.semaphore_wait(
        pltpu.get_barrier_semaphore(),
        2 * HEADS + 3 - same_chunk.astype(jnp.int32) - same_query.astype(jnp.int32),
    )

    def spread(source, landing, number):
        def step(t, carry):
            y2, zh2 = partner(t, y, zh)
            off = lax.rem(z - 2 * zh2 + 11, 8) - 3
            zl2 = (off > 0).astype(jnp.int32)
            turn = jnp.where(off > 0, off - 1, -off)
            x2 = lax.rem(turn + y2 + zh2, 4)
            head = y2 * 4 + zh2
            send(
                source.at[:, pl.ds(pl.multiple_of(head * HEAD_DIM, HEAD_DIM), HEAD_DIM)],
                landing.at[lax.div(t, 4), x],
                send_sem.at[number],
                quarter_sem.at[4 * number + lax.div(t, 8)],
                here,
                (y2, x2 * 8 + 2 * zh2 + zl2, core),
            )
            return carry

        lax.fori_loop(0, HEADS, step, 0)

    def send_queries():
        def step(t, carry):
            y2, zh2 = partner(t, y, zh)
            z2 = 2 * zh2 + lax.rem(y, 2)
            head = y2 * 4 + zh2
            send(
                q_ref.at[:, pl.ds(pl.multiple_of(head * HEAD_DIM, HEAD_DIM), HEAD_DIM)],
                q_out.at[lax.div(y, 2), z],
                send_sem.at[2],
                recv_sem.at[2],
                here,
                (y2, x * 8 + z2, core),
            )
            return carry

        lax.fori_loop(0, HEADS, step, 0)

    def remote(src, dst, sent, received, there):
        return pltpu.make_async_remote_copy(
            src_ref=src,
            dst_ref=dst,
            send_sem=sent,
            recv_sem=received,
            device_id=there,
            device_id_type=MESH,
        )

    def swap(spread_ref, other_ref, number):
        for quarter in range(4):
            part = pl.ds(2 * quarter, 2)
            wait_bytes(spread_ref.at[part], quarter_sem.at[4 * number + quarter])
            remote(
                spread_ref.at[part],
                other_ref.at[part],
                send_sem.at[3 + number],
                recv_sem.at[3 + number],
                at(x, 1 - zl),
            ).start()

    def spot(slot, side):
        source = lax.div(chunk_of(y, x, zh, zl if side == 0 else 1 - zl), 2)
        eighth = lax.rem(3 * (y + 8 - lax.div(slot, GROUP_FRAMES)), 8)
        quarter = lax.rem(zh + 12 - source - eighth, 4)
        return 2 * quarter + lax.div(eighth, 4), lax.rem(slot, GROUP_FRAMES)

    mates = (right, left, lax.rem(x + 2, 4), x)

    def to_mates(side, spread_ref, stage, relay, landing, number):
        def pick(p, carry):
            for mate, x2 in enumerate(mates):
                slot = lists_ref[(2 * x2 + zl) * SLOTS + p]
                stage[side, mate, p] = spread_ref[spot(slot, side)]
            return carry

        lax.fori_loop(0, capacity, pick, 0)
        rows = landing.at[:, chunk_of(y, x, zh, zl if side == 0 else 1 - zl)]
        sent, landed = send_sem.at[5 + number], recv_sem.at[5 + number]
        by = right if side == 0 else left
        passed = relay_sem.at[2 * number + side]
        remote(stage.at[side, 2], relay.at[side], sent, passed, at(by, zl)).start()
        remote(stage.at[side, 0], rows, sent, landed, at(right, zl)).start()
        remote(stage.at[side, 1], rows, sent, landed, at(left, zl)).start()
        pltpu.make_async_copy(stage.at[side, 3], rows, landed).start()

    def pass_on(side, relay, landing, number):
        wait_bytes(relay.at[side], relay_sem.at[2 * number + side])
        owner, there = (left, right) if side == 0 else (right, left)
        rows = landing.at[:, chunk_of(y, owner, zh, zl if side == 0 else 1 - zl)]
        remote(
            relay.at[side], rows, send_sem.at[7 + number], recv_sem.at[5 + number], at(there, zl)
        ).start()

    spread(k_ref, k_spread, 0)
    spread(v_ref, v_spread, 1)
    swap(k_spread, k_other, 0)
    to_mates(0, k_spread, k_stage, k_relay, k_out, 0)
    send_queries()
    swap(v_spread, v_other, 1)
    to_mates(0, v_spread, v_stage, v_relay, v_out, 1)
    wait_bytes(k_other, recv_sem.at[3])
    to_mates(1, k_other, k_stage, k_relay, k_out, 0)
    pass_on(0, k_relay, k_out, 0)
    wait_bytes(v_other, recv_sem.at[4])
    to_mates(1, v_other, v_stage, v_relay, v_out, 1)
    pass_on(0, v_relay, v_out, 1)
    pass_on(1, k_relay, k_out, 0)
    pass_on(1, v_relay, v_out, 1)
    wait_bytes(k_spread, send_sem.at[3])
    wait_bytes(v_spread, send_sem.at[4])

    def wait_sent(number, own_copy):
        @pl.when(own_copy)
        def _():
            wait_bytes(k_ref.at[:, pl.ds(0, (HEADS - 1) * HEAD_DIM)], send_sem.at[number])

        @pl.when(jnp.logical_not(own_copy))
        def _():
            wait_bytes(k_spread, send_sem.at[number])

    own_copy = same_chunk & (lax.rem(y + zh, 4) == x)
    wait_sent(0, own_copy)
    wait_sent(1, own_copy)
    wait_sent(2, same_query)
    for number, stage, relay in ((0, k_stage, k_relay), (1, v_stage, v_relay)):
        wait_bytes(stage.at[:, pl.ds(0, 3)], send_sem.at[5 + number])
        wait_bytes(relay, send_sem.at[7 + number])
    wait_bytes(q_out, recv_sem.at[2])
    wait_bytes(k_out, recv_sem.at[5])
    wait_bytes(v_out, recv_sem.at[6])


def gather(capacity, lists, queries, key_rows, values):
    any_space = pl.BlockSpec(memory_space=pl.ANY)
    pieces = (GROUP_FRAMES, GROUPS, CHUNK, HEAD_DIM)
    picked = (capacity, GROUPS, CHUNK, HEAD_DIM)
    scratch = [(GROUPS, GROUP_FRAMES)] * 4 + [(2, 4, capacity)] * 2 + [(2, capacity)] * 2
    return pl.pallas_call(
        functools.partial(gather_kernel, capacity),
        out_shape=[jax.ShapeDtypeStruct(shape, jnp.bfloat16) for shape in (pieces, picked, picked)],
        in_specs=[pl.BlockSpec(memory_space=pltpu.SMEM), any_space, any_space, any_space],
        out_specs=[any_space] * 3,
        scratch_shapes=[
            *(pltpu.VMEM((*shape, CHUNK, HEAD_DIM), jnp.bfloat16) for shape in scratch),
            pltpu.SemaphoreType.DMA((9,)),
            pltpu.SemaphoreType.DMA((7,)),
            pltpu.SemaphoreType.DMA((4,)),
            pltpu.SemaphoreType.DMA((8,)),
        ],
        compiler_params=pltpu.CompilerParams(
            collective_id=ROOMS.index(capacity), has_side_effects=True, vmem_limit_bytes=40 * 2**20
        ),
    )(lists, queries, key_rows, values)


BLOCK = 256


def attend_kernel(info_ref, q_ref, k_ref, v_ref, o_ref, apart, ones, top, weighted):
    square = (FRAME_PIX, FRAME_PIX)
    apart[...] = jnp.abs(
        lax.broadcasted_iota(jnp.int32, square, 0) - lax.broadcasted_iota(jnp.int32, square, 1)
    )
    ones[...] = jnp.ones_like(ones)

    def tile(own, position, width, first, narrow):
        for block in range(FRAME_PIX // BLOCK):
            rows = pl.ds(block * BLOCK, BLOCK)
            near = pl.ds(block * 128, 384) if narrow else pl.ds(0, FRAME_PIX)
            scores = lax.dot_general(
                q_ref[own, rows, :],
                k_ref[position, near, :],
                (((1,), (1,)), ((), ())),
                preferred_element_type=jnp.float32,
            )
            masked = jnp.where(apart[rows, near] < width, scores * SCALE, -1e30)
            high = jnp.max(masked, axis=1, keepdims=True)
            if first:
                new_top = high
            else:
                old_top = top[rows, :]
                new_top = jnp.maximum(old_top, high)
            weight = jnp.exp2(masked - new_top)
            product = jnp.dot(
                weight.astype(jnp.bfloat16),
                jnp.concatenate([v_ref[position, near, :], ones[near, :]], axis=1),
                preferred_element_type=jnp.float32,
            )
            if first:
                weighted[rows, :] = product
            else:
                weighted[rows, :] = weighted[rows, :] * jnp.exp2(old_top - new_top) + product
            top[rows, :] = new_top

    def one_frame(own, carry):
        code = info_ref[own * SLOTS]
        tile(own, lax.shift_right_logical(code, 10), lax.bitwise_and(code, 1023), True, False)

        def visit(number, inner):
            code = info_ref[own * SLOTS + number]
            position, width = lax.shift_right_logical(code, 10), lax.bitwise_and(code, 1023)

            @pl.when(width > 128)
            def _():
                tile(own, position, width, False, False)

            @pl.when(width <= 128)
            def _():
                tile(own, position, width, False, True)

            return inner

        lax.fori_loop(1, info_ref[GROUP_FRAMES * SLOTS + own], visit, 0)
        o_ref[own] = (weighted[:, :HEAD_DIM] / weighted[:, HEAD_DIM:]).astype(jnp.bfloat16)
        return carry

    lax.fori_loop(0, GROUP_FRAMES, one_frame, 0)


def attend(info, q_local, keys, vals):
    capacity = keys.shape[0]
    vmem = pl.BlockSpec(memory_space=pltpu.VMEM)
    outcome = pl.pallas_call(
        attend_kernel,
        out_shape=jax.ShapeDtypeStruct((GROUP_FRAMES, FRAME_PIX, HEAD_DIM), jnp.bfloat16),
        in_specs=[pl.BlockSpec(memory_space=pltpu.SMEM), vmem, vmem, vmem],
        out_specs=vmem,
        scratch_shapes=[
            pltpu.VMEM((FRAME_PIX, FRAME_PIX), jnp.int32),
            pltpu.VMEM((FRAME_PIX, HEAD_DIM), jnp.bfloat16),
            pltpu.VMEM((FRAME_PIX, 1), jnp.float32),
            pltpu.VMEM((FRAME_PIX, 2 * HEAD_DIM), jnp.float32),
        ],
        compiler_params=pltpu.CompilerParams(vmem_limit_bytes=40 * 2**20),
    )(
        info,
        q_local.reshape(GROUP_FRAMES, FRAME_PIX, HEAD_DIM),
        keys.reshape(capacity, FRAME_PIX, HEAD_DIM),
        vals.reshape(capacity, FRAME_PIX, HEAD_DIM),
    )
    return outcome.reshape(GROUP_FRAMES, GROUPS, CHUNK, HEAD_DIM)


def return_kernel(o_ref, out_ref, send_sem, recv_sem):
    y, x, zh, zl, core = place()
    z = 2 * zh + zl
    here = (y, x * 8 + z, core)
    head = y * 4 + zh
    same = lax.rem(y, 2) == zl

    def greet_senders(t, carry):
        y2, z2 = lax.rem(t, 8), 2 * lax.div(t, 8) + lax.rem(y, 2)

        @pl.when((y2 != y) | (z2 != z))
        def _():
            greet((y2, x * 8 + z2, core))

        return carry

    lax.fori_loop(0, HEADS, greet_senders, 0)
    pl.semaphore_wait(pltpu.get_barrier_semaphore(), HEADS - same.astype(jnp.int32))

    def step(t, carry):
        number = lax.rem(lax.div(y, 2) + t + lax.div(t, 8), 4)
        y2 = 2 * number + zl
        z2 = lax.rem(z + 3 * t, 8)
        send(
            o_ref.at[number, z2],
            out_ref.at[head],
            send_sem,
            recv_sem,
            here,
            (y2, x * 8 + z2, core),
        )
        return carry

    lax.fori_loop(0, HEADS, step, 0)
    sent = out_ref.at[pl.ds(0, HEADS - 1)]

    @pl.when(same)
    def _():
        wait_bytes(sent, send_sem)

    @pl.when(jnp.logical_not(same))
    def _():
        wait_bytes(out_ref, send_sem)

    wait_bytes(out_ref, recv_sem)


def send_back(outcome):
    any_space = pl.BlockSpec(memory_space=pl.ANY)
    by_head = pl.pallas_call(
        return_kernel,
        out_shape=jax.ShapeDtypeStruct((HEADS, CHUNK, HEAD_DIM), jnp.bfloat16),
        in_specs=[any_space],
        out_specs=any_space,
        scratch_shapes=[pltpu.SemaphoreType.DMA, pltpu.SemaphoreType.DMA],
        compiler_params=pltpu.CompilerParams(collective_id=len(ROOMS), has_side_effects=True),
    )(outcome)
    return by_head.transpose(1, 0, 2).reshape(CHUNK, HEADS * HEAD_DIM)


def on_device(queries, key_rows, values, slot_frame, radial_tiles):
    on_query = slot_frame[:, None] == radial_tiles[None, :, 0]
    on_key = slot_frame[:, None] == radial_tiles[None, :, 1]
    slot_width = jnp.dot(
        on_query.astype(jnp.int32) * radial_tiles[None, :, 2], on_key.astype(jnp.int32).T
    )
    by_group = slot_width.reshape(GROUP_FRAMES, 2, GROUP_FRAMES, SLOTS).transpose(2, 1, 0, 3)
    by_group = by_group.reshape(GROUPS, GROUP_FRAMES, SLOTS)
    needed = jnp.max(by_group, axis=1) > 0
    slots = jnp.arange(SLOTS, dtype=jnp.int32)
    before = (slots[:, None] < slots[None, :]).astype(jnp.int32)
    rank = jnp.dot(needed.astype(jnp.int32), before)
    chosen = needed[:, :, None] & (rank[:, :, None] == slots[None, None, :])
    lists = jnp.sum(jnp.where(chosen, slots[None, :, None], 0), axis=1)
    most = jnp.max(jnp.sum(needed.astype(jnp.int32), axis=1))
    y, x, zh, zl, core = place()
    group = 2 * x + zl
    my_width = lax.dynamic_index_in_dim(by_group, group, 0, False)
    my_rank = lax.dynamic_index_in_dim(rank, group, 0, False)
    own = slots[None, :] == (GROUP_FRAMES * (2 * slots[:GROUP_FRAMES] + zl) + x)[:, None]
    others = (my_width > 0) & jnp.logical_not(own)
    order = jnp.where(own, 0, 1 + jnp.dot(others.astype(jnp.int32), before))
    here = (own | others)[:, :, None] & (order[:, :, None] == slots[None, None, :])
    codes = jnp.sum(jnp.where(here, (my_rank[None, :] * 1024 + my_width)[:, :, None], 0), axis=1)
    counts = 1 + jnp.sum(others.astype(jnp.int32), axis=1)
    info = jnp.concatenate([codes.reshape(-1), counts])

    def run(capacity):
        def branch(lists, info, queries, key_rows, values):
            q_local, keys, vals = gather(capacity, lists, queries, key_rows, values)
            return attend(info, q_local, keys, vals)

        return branch

    index = sum((most > room).astype(jnp.int32) for room in ROOMS[:-1])
    outcome = lax.switch(
        index, [run(room) for room in ROOMS], lists.reshape(-1), info, queries, key_rows, values
    )
    return send_back(outcome)


def solution(mesh):
    placed = (
        P(("rep", "frame", "head"), None),
        P(("rep", "frame", "head"), None),
        P(("rep", "frame", "head"), None),
        P(),
        P(),
    )
    return jax.shard_map(
        on_device,
        mesh=mesh,
        in_specs=placed,
        out_specs=P(("rep", "frame", "head"), None),
        check_vma=False,
    )
```

time: 341 us -> 130 us (0.38)
  the two profiles are of different devices: /device:TPU:64 before, /device:TPU:2 now
where the time goes in v1:
time: 130 us; the launch traced here: 129 us
  Pallas kernels  122 us (94%)
  local copies, waits for them, and re-layouts  2.9 us (2%)
  between operations  2 us (2%)
  other arithmetic  1.33 us (1%)
    pallas_call x1, Pallas kernels, gather(): pl.pallas_call(functools.partial(gather_kernel, capacity), out_shape=[jax...  86 us
    pallas_call x1, Pallas kernels, send_back(): pl.pallas_call(return_kernel, out_shape=jax.ShapeDtypeStruct((HEADS, CHUN...  25.7 us
    pallas_call x1, Pallas kernels, attend(): pl.pallas_call(attend_kernel, out_shape=jax.ShapeDtypeStruct((GROUP_FRAME...  10.1 us

profile of v1, /device:TPU:2, one launch (start us, length us, event | category | flops | bytes accessed | tf_op | source)
XLA Modules:
  0.0 129.3 jit_solution(10905378859667300261)
XLA Ops:
  0.0 0.8 fusion.18
  0.8 0.9 fusion.3
  1.8 0.1 convert_reduce_fusion
  1.9 0.6 reduce_max.19
  4.5 0.1 fusion.13
  4.6 0.1 convert_reduce_fusion.1
  4.7 0.1 fusion
  4.9 0.1 fusion.7
  5.0 0.1 select_reduce_fusion.1
  5.2 0.1 reshape.124
  5.3 0.1 select_reduce_fusion
  5.4 0.1 reshape.122
  5.5 96.1 %conditional.1 = (bf16[4,512,128]{2,1,0:T(8,128)(2,1)S(1)}) conditional(s32[]{:T(128)} %clamp.3, (s32[256]{0:T(256)S(1)}, bf16[64,4096]{1,0:T(8,128)(2,1)}, bf16[64,4096]{1,0:T(8,128)(2,1)}, bf16[64,4096]{1,0:T(8,128)(2,1)}, s32[132]{0:T(256)S(1)}) %tuple.22, (s32[256]{0:T(256)S(1)}, bf16[64,4096]{1,0:T(8,128)(2,1)}, ...), branch_computations={%region_6.7_spmd, %region_7.8_spmd, %region_8.9_spmd, %region_9.10... | conditional | bytes 8 | solution.py:463
  5.5 86.0 %branch_0_fun.2 = (bf16[4,8,64,128]{3,2,1,0:T(8,128)(2,1)S(1)}, bf16[12,8,64,128]{3,2,1,0:T(8,128)(2,1)S(1)}, bf16[12,8,64,128]{3,2,1,0:T(8,128)(2,1)S(1)}) custom-call(s32[256]{0:T(256)S(1)} %get-tuple-element.52.lists_ref, bf16[64,4096]{1,0:T(8,128)(2,1)} %get-tuple-element.53.q_ref, bf16[64,4096]{1,0:T(8,128)(2,1)} %get-tuple-element.54.k_ref, ...), custom_call_target="tpu_custom_call" | custom-call | tf_op jit(solution)/shard_map/cond/branch_0_fun/pallas_call | solution.py:262
  91.5 10.1 %branch_0_fun.3 = bf16[4,512,128]{2,1,0:T(8,128)(2,1)S(1)} custom-call(s32[132]{0:T(256)S(1)} %get-tuple-element.50.info_ref, bf16[4,512,128]{2,1,0:T(8,128)(2,1)S(1)} %bitcast.44, bf16[12,512,128]{2,1,0:T(8,128)(2,1)S(1)} %bitcast.42, bf16[12,512,128]{2,1,0:T(8,128)(2,1)S(1)} %bitcast.43), custom_call_target="tpu_custom_call" | custom-call | tf_op jit(solution)/shard_map/cond/branch_0_fun/pallas_call | solution.py:347
  101.6 25.7 %shard_map.55 = bf16[32,64,128]{2,1,0:T(8,128)(2,1)} custom-call(bf16[4,8,64,128]{3,2,1,0:T(8,128)(2,1)S(1)} %bitcast.48), custom_call_target="tpu_custom_call" | custom-call | tf_op jit(solution)/shard_map/pallas_call | solution.py:417
  127.4 1.9 %copy_bitcast_fusion = bf16[64,4096]{1,0:T(8,128)(2,1)} fusion(bf16[32,64,128]{2,1,0:T(8,128)(2,1)} %shard_map.55), kind=kLoop, calls=%fused_computation.2 | loop fusion | bytes 1048576 | tf_op jit(solution)/shard_map/reshape | solution.py:425
  (10 shorter events, 0.1 us)

commit v2 on v1

--- a/solution.py
+++ b/solution.py
@@ -133,7 +133,7 @@
             head = y2 * 4 + zh2
             send(
                 source.at[:, pl.ds(pl.multiple_of(head * HEAD_DIM, HEAD_DIM), HEAD_DIM)],
-                landing.at[lax.div(t, 4), x],
+                landing.at[lax.div(t, 4) * 4 + x],
                 send_sem.at[number],
                 quarter_sem.at[4 * number + lax.div(t, 8)],
                 here,
@@ -172,7 +172,7 @@
 
     def swap(spread_ref, other_ref, number):
         for quarter in range(4):
-            part = pl.ds(2 * quarter, 2)
+            part = pl.ds(8 * quarter, 8)
             wait_bytes(spread_ref.at[part], quarter_sem.at[4 * number + quarter])
             remote(
                 spread_ref.at[part],
@@ -182,38 +182,41 @@
                 at(x, 1 - zl),
             ).start()
 
-    def spot(slot, side):
-        source = lax.div(chunk_of(y, x, zh, zl if side == 0 else 1 - zl), 2)
-        eighth = lax.rem(3 * (y + 8 - lax.div(slot, GROUP_FRAMES)), 8)
-        quarter = lax.rem(zh + 12 - source - eighth, 4)
-        return 2 * quarter + lax.div(eighth, 4), lax.rem(slot, GROUP_FRAMES)
-
+    middle = capacity // 2
+    halves = (
+        (pl.ds(0, middle), right, left),
+        (pl.ds(middle, capacity - middle), left, right),
+    )
     mates = (right, left, lax.rem(x + 2, 4), x)
 
     def to_mates(side, spread_ref, stage, relay, landing, number):
         def pick(p, carry):
             for mate, x2 in enumerate(mates):
-                slot = lists_ref[(2 * x2 + zl) * SLOTS + p]
-                stage[side, mate, p] = spread_ref[spot(slot, side)]
+                stage[side, mate, p] = spread_ref[lists_ref[side * 256 + (2 * x2 + zl) * SLOTS + p]]
             return carry
 
         lax.fori_loop(0, capacity, pick, 0)
         rows = landing.at[:, chunk_of(y, x, zh, zl if side == 0 else 1 - zl)]
         sent, landed = send_sem.at[5 + number], recv_sem.at[5 + number]
-        by = right if side == 0 else left
-        passed = relay_sem.at[2 * number + side]
-        remote(stage.at[side, 2], relay.at[side], sent, passed, at(by, zl)).start()
+        for half, (part, by, _) in enumerate(halves):
+            remote(
+                stage.at[side, 2, part],
+                relay.at[side, part],
+                sent,
+                relay_sem.at[4 * number + 2 * side + half],
+                at(by, zl),
+            ).start()
         remote(stage.at[side, 0], rows, sent, landed, at(right, zl)).start()
         remote(stage.at[side, 1], rows, sent, landed, at(left, zl)).start()
         pltpu.make_async_copy(stage.at[side, 3], rows, landed).start()
 
     def pass_on(side, relay, landing, number):
-        wait_bytes(relay.at[side], relay_sem.at[2 * number + side])
-        owner, there = (left, right) if side == 0 else (right, left)
-        rows = landing.at[:, chunk_of(y, owner, zh, zl if side == 0 else 1 - zl)]
-        remote(
-            relay.at[side], rows, send_sem.at[7 + number], recv_sem.at[5 + number], at(there, zl)
-        ).start()
+        for half, (part, there, owner) in enumerate(halves):
+            wait_bytes(relay.at[side, part], relay_sem.at[4 * number + 2 * side + half])
+            rows = landing.at[part, chunk_of(y, owner, zh, zl if side == 0 else 1 - zl)]
+            remote(
+                relay.at[side, part], rows, send_sem.at[7 + number], recv_sem.at[5 + number], at(there, zl)
+            ).start()
 
     spread(k_ref, k_spread, 0)
     spread(v_ref, v_spread, 1)
@@ -258,7 +261,7 @@
     any_space = pl.BlockSpec(memory_space=pl.ANY)
     pieces = (GROUP_FRAMES, GROUPS, CHUNK, HEAD_DIM)
     picked = (capacity, GROUPS, CHUNK, HEAD_DIM)
-    scratch = [(GROUPS, GROUP_FRAMES)] * 4 + [(2, 4, capacity)] * 2 + [(2, capacity)] * 2
+    scratch = [(SLOTS,)] * 4 + [(2, 4, capacity)] * 2 + [(2, capacity)] * 2
     return pl.pallas_call(
         functools.partial(gather_kernel, capacity),
         out_shape=[jax.ShapeDtypeStruct(shape, jnp.bfloat16) for shape in (pieces, picked, picked)],
@@ -268,7 +271,7 @@
             *(pltpu.VMEM((*shape, CHUNK, HEAD_DIM), jnp.bfloat16) for shape in scratch),
             pltpu.SemaphoreType.DMA((9,)),
             pltpu.SemaphoreType.DMA((7,)),
-            pltpu.SemaphoreType.DMA((4,)),
+            pltpu.SemaphoreType.DMA((8,)),
             pltpu.SemaphoreType.DMA((8,)),
         ],
         compiler_params=pltpu.CompilerParams(
@@ -277,7 +280,7 @@
     )(lists, queries, key_rows, values)
 
 
-BLOCK = 256
+BLOCK = 128
 
 
 def attend_kernel(info_ref, q_ref, k_ref, v_ref, o_ref, apart, ones, top, weighted):
@@ -287,10 +290,11 @@
     )
     ones[...] = jnp.ones_like(ones)
 
-    def tile(own, position, width, first, narrow):
+    def tile(own, position, width, first, reach):
         for block in range(FRAME_PIX // BLOCK):
             rows = pl.ds(block * BLOCK, BLOCK)
-            near = pl.ds(block * 128, 384) if narrow else pl.ds(0, FRAME_PIX)
+            low = max(0, block * BLOCK - reach)
+            near = pl.ds(low, min(FRAME_PIX, (block + 1) * BLOCK + reach) - low)
             scores = lax.dot_general(
                 q_ref[own, rows, :],
                 k_ref[position, near, :],
@@ -318,19 +322,23 @@
 
     def one_frame(own, carry):
         code = info_ref[own * SLOTS]
-        tile(own, lax.shift_right_logical(code, 10), lax.bitwise_and(code, 1023), True, False)
+        tile(own, lax.shift_right_logical(code, 10), lax.bitwise_and(code, 1023), True, FRAME_PIX)
 
         def visit(number, inner):
             code = info_ref[own * SLOTS + number]
             position, width = lax.shift_right_logical(code, 10), lax.bitwise_and(code, 1023)
 
-            @pl.when(width > 128)
+            @pl.when(width > 256)
             def _():
-                tile(own, position, width, False, False)
+                tile(own, position, width, False, FRAME_PIX)
+
+            @pl.when((width > 128) & (width <= 256))
+            def _():
+                tile(own, position, width, False, 256)
 
             @pl.when(width <= 128)
             def _():
-                tile(own, position, width, False, True)
+                tile(own, position, width, False, 128)
 
             return inner
 
@@ -425,32 +433,87 @@
     return by_head.transpose(1, 0, 2).reshape(CHUNK, HEADS * HEAD_DIM)
 
 
+def plan_kernel(slot_ref, tiles_ref, lists_ref, info_ref, index_ref):
+    y, x, zh, zl, core = place()
+    half, single = jnp.bfloat16, jnp.float32
+
+    def flags(condition):
+        return jnp.where(condition, 1.0, 0.0)
+
+    def times(left, right):
+        return jnp.dot(left.astype(half), right.astype(half), preferred_element_type=single)
+
+    def across(left, right):
+        return lax.dot_general(
+            left.astype(half), right.astype(half), (((1,), (1,)), ((), ())), preferred_element_type=single
+        )
+
+    def iota(rows, columns, dimension):
+        return lax.broadcasted_iota(jnp.int32, (rows, columns), dimension)
+
+    diagonal = iota(SLOTS, SLOTS, 0) == iota(SLOTS, SLOTS, 1)
+    slots = jnp.sum(jnp.where(diagonal, slot_ref[...], 0), axis=1, keepdims=True)
+    on_query = tiles_ref[0:1, :] == slots
+    on_key = flags(tiles_ref[1:2, :] == slots)
+    widths = tiles_ref[2:3, :]
+    coarse = across(jnp.where(on_query, lax.shift_right_logical(widths, 4).astype(single), 0.0), on_key)
+    fine = across(jnp.where(on_query, lax.bitwise_and(widths, 15).astype(single), 0.0), on_key)
+    slot = iota(GROUPS, SLOTS, 1)
+    group = 2 * lax.bitwise_and(slot, 3) + lax.bitwise_and(lax.shift_right_logical(slot, 2), 1)
+    in_group = flags(group == iota(GROUPS, SLOTS, 0))
+    needed = flags(times(in_group, flags(coarse + fine > 0)) > 0)
+    before = flags(iota(SLOTS, SLOTS, 0) < iota(SLOTS, SLOTS, 1))
+    rank = times(needed, before)
+    order = iota(SLOTS, SLOTS, 0).astype(single)
+    picks = [
+        flags(rank[g : g + 1] == order) * needed[g : g + 1] for g in range(GROUPS)
+    ]
+    number = iota(1, SLOTS, 1)
+    for side, low in ((0, zl), (1, 1 - zl)):
+        source = lax.div(chunk_of(y, x, zh, low), 2)
+        eighth = lax.bitwise_and(3 * (y + 8 - lax.shift_right_logical(number, 2)), 7)
+        quarter = lax.bitwise_and(zh + 12 - source - eighth, 3)
+        spot = quarter * 8 + lax.bitwise_and(eighth, 4) + lax.bitwise_and(number, 3)
+        found = across(spot.astype(single), jnp.concatenate(picks, axis=0))
+        lists_ref[:, side * 256 : side * 256 + 256] = found.astype(jnp.int32)
+    most = jnp.max(jnp.sum(needed, axis=1, keepdims=True), axis=0, keepdims=True)
+    index = sum(flags(most > room) for room in ROOMS[:-1])
+    index_ref[...] = jnp.broadcast_to(index, (1, 128)).astype(jnp.int32)
+    query = iota(GROUP_FRAMES, SLOTS, 0)
+    own = flags(iota(GROUP_FRAMES, SLOTS, 1) == GROUP_FRAMES * (2 * query + zl) + x)
+    my_coarse, my_fine = times(own, coarse), times(own, fine)
+    others = flags(my_coarse + my_fine > 0) * (1.0 - own)
+    turn = (1.0 + times(others, before)) * (1.0 - own)
+    at = [
+        flags(turn[q : q + 1] == order) * (own + others)[q : q + 1] for q in range(GROUP_FRAMES)
+    ]
+    ones = jnp.ones((1, SLOTS), single)
+    my_rank = times(flags(iota(1, GROUPS, 1) == 2 * x + zl), rank)
+    place_of = across(my_rank, jnp.concatenate(at, axis=0))
+    coarse_of = across(
+        ones, jnp.concatenate([at[q] * my_coarse[q : q + 1] for q in range(GROUP_FRAMES)], axis=0)
+    )
+    fine_of = across(
+        ones, jnp.concatenate([at[q] * my_fine[q : q + 1] for q in range(GROUP_FRAMES)], axis=0)
+    )
+    info_ref[:, :128] = (place_of * 1024 + coarse_of * 16 + fine_of).astype(jnp.int32)
+    padded = jnp.concatenate([others, jnp.zeros((128 - GROUP_FRAMES, SLOTS), single)], axis=0)
+    info_ref[:, 128:] = 1 + across(ones, padded).astype(jnp.int32)
+
+
+def plan(slot_frame, radial_tiles):
+    vmem = pl.BlockSpec(memory_space=pltpu.VMEM)
+    lists, info, index = pl.pallas_call(
+        plan_kernel,
+        out_shape=[jax.ShapeDtypeStruct((1, size), jnp.int32) for size in (512, 256, 128)],
+        in_specs=[vmem] * 2,
+        out_specs=[vmem] * 3,
+    )(slot_frame.reshape(1, SLOTS), radial_tiles.T)
+    return lists.reshape(-1), info.reshape(-1), index[0, 0]
+
+
 def on_device(queries, key_rows, values, slot_frame, radial_tiles):
-    on_query = slot_frame[:, None] == radial_tiles[None, :, 0]
-    on_key = slot_frame[:, None] == radial_tiles[None, :, 1]
-    slot_width = jnp.dot(
-        on_query.astype(jnp.int32) * radial_tiles[None, :, 2], on_key.astype(jnp.int32).T
-    )
-    by_group = slot_width.reshape(GROUP_FRAMES, 2, GROUP_FRAMES, SLOTS).transpose(2, 1, 0, 3)
-    by_group = by_group.reshape(GROUPS, GROUP_FRAMES, SLOTS)
-    needed = jnp.max(by_group, axis=1) > 0
-    slots = jnp.arange(SLOTS, dtype=jnp.int32)
-    before = (slots[:, None] < slots[None, :]).astype(jnp.int32)
-    rank = jnp.dot(needed.astype(jnp.int32), before)
-    chosen = needed[:, :, None] & (rank[:, :, None] == slots[None, None, :])
-    lists = jnp.sum(jnp.where(chosen, slots[None, :, None], 0), axis=1)
-    most = jnp.max(jnp.sum(needed.astype(jnp.int32), axis=1))
-    y, x, zh, zl, core = place()
-    group = 2 * x + zl
-    my_width = lax.dynamic_index_in_dim(by_group, group, 0, False)
-    my_rank = lax.dynamic_index_in_dim(rank, group, 0, False)
-    own = slots[None, :] == (GROUP_FRAMES * (2 * slots[:GROUP_FRAMES] + zl) + x)[:, None]
-    others = (my_width > 0) & jnp.logical_not(own)
-    order = jnp.where(own, 0, 1 + jnp.dot(others.astype(jnp.int32), before))
-    here = (own | others)[:, :, None] & (order[:, :, None] == slots[None, None, :])
-    codes = jnp.sum(jnp.where(here, (my_rank[None, :] * 1024 + my_width)[:, :, None], 0), axis=1)
-    counts = 1 + jnp.sum(others.astype(jnp.int32), axis=1)
-    info = jnp.concatenate([codes.reshape(-1), counts])
+    lists, info, index = plan(slot_frame, radial_tiles)
 
     def run(capacity):
         def branch(lists, info, queries, key_rows, values):
@@ -459,9 +522,8 @@
 
         return branch
 
-    index = sum((most > room).astype(jnp.int32) for room in ROOMS[:-1])
     outcome = lax.switch(
-        index, [run(room) for room in ROOMS], lists.reshape(-1), info, queries, key_rows, values
+        index, [run(room) for room in ROOMS], lists, info, queries, key_rows, values
     )
     return send_back(outcome)
 

time: 130 us -> 125 us (0.962)
  other arithmetic: 1.33 us -> 0 us
  between operations: 2 us -> 0.67 us
    pallas_call x1, Pallas kernels: 86 us -> 81.4 us  [gather(): pl.pallas_call(functools.partial(gather_kernel, capacity), out_shape=[jax...]
    pallas_call x1, Pallas kernels: 10.1 us -> 12.9 us  [attend(): pl.pallas_call(attend_kernel, out_shape=jax.ShapeDtypeStruct((GROUP_FRAME...]
    pallas_call x0 -> x1, Pallas kernels: none -> 1.83 us  [plan(): pl.pallas_call(plan_kernel, out_shape=[jax.ShapeDtypeStruct((1, size), jn...]
where the time goes in v2:
time: 125 us
  Pallas kernels  122 us (98%)
  local copies, waits for them, and re-layouts  1.9 us (2%)
    pallas_call x1, Pallas kernels, gather(): pl.pallas_call(functools.partial(gather_kernel, capacity), out_shape=[jax...  81.4 us
    pallas_call x1, Pallas kernels, send_back(): pl.pallas_call(return_kernel, out_shape=jax.ShapeDtypeStruct((HEADS, CHUN...  25.6 us
    pallas_call x1, Pallas kernels, attend(): pl.pallas_call(attend_kernel, out_shape=jax.ShapeDtypeStruct((GROUP_FRAME...  12.9 us

profile of v2, /device:TPU:2, one launch (start us, length us, event | category | flops | bytes accessed | tf_op | source)
XLA Modules:
  0.0 124.5 jit_solution(6045613446541718085)
XLA Ops:
  0.0 1.8 %shard_map.55 = (s32[1,512]{1,0:T(1,128)S(1)}, s32[1,256]{1,0:T(1,128)S(1)}, s32[1,128]{1,0:T(1,128)}) custom-call(s32[1,32]{1,0:T(1,128)} %bitcast.47, s32[3,160]{1,0:T(4,128)} %bitcast.46), custom_call_target="tpu_custom_call" | custom-call | tf_op jit(solution)/shard_map/pallas_call | solution.py:506
  2.5 94.5 %conditional.1 = (bf16[4,512,128]{2,1,0:T(8,128)(2,1)S(1)}) conditional(s32[]{:T(128)} %bitcast.14, (s32[512]{0:T(512)S(1)}, bf16[64,4096]{1,0:T(8,128)(2,1)}, bf16[64,4096]{1,0:T(8,128)(2,1)}, bf16[64,4096]{1,0:T(8,128)(2,1)}, s32[256]{0:T(256)S(1)}) %tuple.31, (s32[512]{0:T(512)S(1)}, bf16[64,4096]{1,0:T(8,128)(2,1)}, ...), branch_computations={%region_0.0_spmd, %region_1.0_spmd, %region_2.0_spmd, %region_3.0_... | conditional | bytes 8 | solution.py:525
  2.5 81.4 %branch_0_fun.2 = (bf16[4,8,64,128]{3,2,1,0:T(8,128)(2,1)S(1)}, bf16[12,8,64,128]{3,2,1,0:T(8,128)(2,1)S(1)}, bf16[12,8,64,128]{3,2,1,0:T(8,128)(2,1)S(1)}) custom-call(s32[512]{0:T(512)S(1)} %get-tuple-element.52.lists_ref, bf16[64,4096]{1,0:T(8,128)(2,1)} %get-tuple-element.53.q_ref, bf16[64,4096]{1,0:T(8,128)(2,1)} %get-tuple-element.54.k_ref, ...), custom_call_target="tpu_custom_call" | custom-call | tf_op jit(solution)/shard_map/cond/branch_0_fun/pallas_call | solution.py:265
  83.9 12.9 %branch_0_fun.3 = bf16[4,512,128]{2,1,0:T(8,128)(2,1)S(1)} custom-call(s32[256]{0:T(256)S(1)} %get-tuple-element.50.info_ref, bf16[4,512,128]{2,1,0:T(8,128)(2,1)S(1)} %bitcast.33, bf16[12,512,128]{2,1,0:T(8,128)(2,1)S(1)} %bitcast.31, bf16[12,512,128]{2,1,0:T(8,128)(2,1)S(1)} %bitcast.32), custom_call_target="tpu_custom_call" | custom-call | tf_op jit(solution)/shard_map/cond/branch_0_fun/pallas_call | solution.py:355
  97.0 25.6 %shard_map.56 = bf16[32,64,128]{2,1,0:T(8,128)(2,1)} custom-call(bf16[4,8,64,128]{3,2,1,0:T(8,128)(2,1)S(1)} %bitcast.37), custom_call_target="tpu_custom_call" | custom-call | tf_op jit(solution)/shard_map/pallas_call | solution.py:425
  122.6 1.9 %copy_bitcast_fusion = bf16[64,4096]{1,0:T(8,128)(2,1)} fusion(bf16[32,64,128]{2,1,0:T(8,128)(2,1)} %shard_map.56), kind=kLoop, calls=%fused_computation | loop fusion | bytes 1048576 | tf_op jit(solution)/shard_map/reshape | solution.py:433

commit v3 on v2

--- a/solution.py
+++ b/solution.py
@@ -28,27 +28,27 @@
     return y, x, lax.div(z, 2), lax.rem(z, 2), lax.axis_index("rep")
 
 
-def partner(t, y, zh):
-    return lax.rem(y + 3 * t, 8), lax.rem(zh + t + lax.div(t, 8), 4)
-
-
-def send(src, dst, send_sem, recv_sem, here, there):
+def remote(src, dst, sent, received, there):
+    return pltpu.make_async_remote_copy(
+        src_ref=src,
+        dst_ref=dst,
+        send_sem=sent,
+        recv_sem=received,
+        device_id=there,
+        device_id_type=MESH,
+    )
+
+
+def send(src, dst, sent, received, here, there):
     same = (here[0] == there[0]) & (here[1] == there[1])
 
     @pl.when(same)
     def _():
-        pltpu.make_async_copy(src, dst, recv_sem).start()
+        pltpu.make_async_copy(src, dst, received).start()
 
     @pl.when(jnp.logical_not(same))
     def _():
-        pltpu.make_async_remote_copy(
-            src_ref=src,
-            dst_ref=dst,
-            send_sem=send_sem,
-            recv_sem=recv_sem,
-            device_id=there,
-            device_id_type=MESH,
-        ).start()
+        remote(src, dst, sent, received, there).start()
 
 
 def greet(there):
@@ -100,22 +100,31 @@
     same_chunk = chunk == z
     same_query = lax.rem(y, 2) == zl
 
-    def greet_senders(t, carry):
-        y1, x1 = lax.rem(t, 8), lax.div(t, 8)
-
-        @pl.when((y1 != y) | (x1 != x) | (chunk != z))
-        def _():
-            greet((y1, x1 * 8 + chunk, core))
-
-        y2, z2 = 2 * lax.rem(t, 4) + zl, lax.div(t, 4)
-
-        @pl.when((y2 != y) | (z2 != z))
-        def _():
-            greet((y2, x * 8 + z2, core))
-
+    xs = [lax.rem(x + dx, 4) * 8 + chunk for dx in range(4)]
+    ys = [2 * number + zl for number in range(4)]
+
+    def greet_senders(i, carry):
+        y1, xz1 = lax.rem(y + i, 8), x * 8 + lax.rem(z + i, 8)
+        for xz in xs:
+            greet((y1, xz, core))
+        for y2 in ys:
+            greet((y2, xz1, core))
         return carry
 
-    lax.fori_loop(0, HEADS, greet_senders, 0)
+    lax.fori_loop(1, 8, greet_senders, 0)
+    for xz in xs[1:]:
+        greet((y, xz, core))
+
+    @pl.when(jnp.logical_not(same_chunk))
+    def _():
+        greet((y, xs[0], core))
+
+    for y2 in ys:
+
+        @pl.when(y2 != y)
+        def _(y2=y2):
+            greet((y2, x * 8 + z, core))
+
     for mate in (at(right, zl), at(left, zl), at(x, 1 - zl)):
         greet(mate)
     pl.semaphore_wait(
@@ -123,52 +132,47 @@
         2 * HEADS + 3 - same_chunk.astype(jnp.int32) - same_query.astype(jnp.int32),
     )
 
+    planes = [lax.rem(y + 3 * e, 8) for e in range(8)]
+    own_copy = same_chunk
+
+    def columns(source, head):
+        return source.at[:, pl.ds(pl.multiple_of(head * HEAD_DIM, HEAD_DIM), HEAD_DIM)]
+
     def spread(source, landing, number):
-        def step(t, carry):
-            y2, zh2 = partner(t, y, zh)
-            off = lax.rem(z - 2 * zh2 + 11, 8) - 3
-            zl2 = (off > 0).astype(jnp.int32)
-            turn = jnp.where(off > 0, off - 1, -off)
-            x2 = lax.rem(turn + y2 + zh2, 4)
-            head = y2 * 4 + zh2
-            send(
-                source.at[:, pl.ds(pl.multiple_of(head * HEAD_DIM, HEAD_DIM), HEAD_DIM)],
-                landing.at[lax.div(t, 4) * 4 + x],
-                send_sem.at[number],
-                quarter_sem.at[4 * number + lax.div(t, 8)],
-                here,
-                (y2, x2 * 8 + 2 * zh2 + zl2, core),
-            )
+        def step(quarter, carry):
+            zhs = [lax.rem(zh + quarter + r, 4) for r in range(4)]
+            offs = [lax.rem(z - 2 * zh2 + 11, 8) - 3 for zh2 in zhs]
+            lows = [2 * zh2 + (off > 0).astype(jnp.int32) for zh2, off in zip(zhs, offs)]
+            turns = [jnp.where(off > 0, off - 1, -off) + zh2 for off, zh2 in zip(offs, zhs)]
+            sent, received = send_sem.at[number], quarter_sem.at[4 * number + quarter]
+            for e, y2 in enumerate(planes):
+                piece = columns(source, y2 * 4 + zhs[e % 4])
+                rows = landing.at[8 * quarter + e // 4 * 4 + x]
+                there = (y2, lax.rem(turns[e % 4] + y2, 4) * 8 + lows[e % 4], core)
+                if e == 0:
+                    send(piece, rows, sent, received, here, there)
+                else:
+                    remote(piece, rows, sent, received, there).start()
             return carry
 
-        lax.fori_loop(0, HEADS, step, 0)
+        lax.fori_loop(0, 4, step, 0)
 
     def send_queries():
-        def step(t, carry):
-            y2, zh2 = partner(t, y, zh)
-            z2 = 2 * zh2 + lax.rem(y, 2)
-            head = y2 * 4 + zh2
-            send(
-                q_ref.at[:, pl.ds(pl.multiple_of(head * HEAD_DIM, HEAD_DIM), HEAD_DIM)],
-                q_out.at[lax.div(y, 2), z],
-                send_sem.at[2],
-                recv_sem.at[2],
-                here,
-                (y2, x * 8 + z2, core),
-            )
+        rows = q_out.at[lax.div(y, 2), z]
+        odd = x * 8 + lax.rem(y, 2)
+
+        def step(quarter, carry):
+            zhs = [lax.rem(zh + quarter + r, 4) for r in range(4)]
+            for e, y2 in enumerate(planes):
+                piece = columns(q_ref, y2 * 4 + zhs[e % 4])
+                there = (y2, 2 * zhs[e % 4] + odd, core)
+                if e == 0:
+                    send(piece, rows, send_sem.at[2], recv_sem.at[2], here, there)
+                else:
+                    remote(piece, rows, send_sem.at[2], recv_sem.at[2], there).start()
             return carry
 
-        lax.fori_loop(0, HEADS, step, 0)
-
-    def remote(src, dst, sent, received, there):
-        return pltpu.make_async_remote_copy(
-            src_ref=src,
-            dst_ref=dst,
-            send_sem=sent,
-            recv_sem=received,
-            device_id=there,
-            device_id_type=MESH,
-        )
+        lax.fori_loop(0, 4, step, 0)
 
     def swap(spread_ref, other_ref, number):
         for quarter in range(4):
@@ -188,11 +192,12 @@
         (pl.ds(middle, capacity - middle), left, right),
     )
     mates = (right, left, lax.rem(x + 2, 4), x)
+    bases = [(2 * x2 + zl) * SLOTS for x2 in mates]
 
     def to_mates(side, spread_ref, stage, relay, landing, number):
         def pick(p, carry):
-            for mate, x2 in enumerate(mates):
-                stage[side, mate, p] = spread_ref[lists_ref[side * 256 + (2 * x2 + zl) * SLOTS + p]]
+            for mate, base in enumerate(bases):
+                stage[side, mate, p] = spread_ref[lists_ref[side * 256 + base + p]]
             return carry
 
         lax.fori_loop(0, capacity, pick, 0)
@@ -245,7 +250,6 @@
         def _():
             wait_bytes(k_spread, send_sem.at[number])
 
-    own_copy = same_chunk & (lax.rem(y + zh, 4) == x)
     wait_sent(0, own_copy)
     wait_sent(1, own_copy)
     wait_sent(2, same_query)
@@ -380,33 +384,37 @@
     head = y * 4 + zh
     same = lax.rem(y, 2) == zl
 
-    def greet_senders(t, carry):
-        y2, z2 = lax.rem(t, 8), 2 * lax.div(t, 8) + lax.rem(y, 2)
-
-        @pl.when((y2 != y) | (z2 != z))
-        def _():
-            greet((y2, x * 8 + z2, core))
-
+    zs = [x * 8 + 2 * number + lax.rem(y, 2) for number in range(4)]
+
+    def greet_senders(i, carry):
+        y1 = lax.rem(y + i, 8)
+        for xz in zs:
+            greet((y1, xz, core))
         return carry
 
-    lax.fori_loop(0, HEADS, greet_senders, 0)
+    lax.fori_loop(1, 8, greet_senders, 0)
+    for xz in zs:
+
+        @pl.when(xz != x * 8 + z)
+        def _(xz=xz):
+            greet((y, xz, core))
+
     pl.semaphore_wait(pltpu.get_barrier_semaphore(), HEADS - same.astype(jnp.int32))
-
-    def step(t, carry):
-        number = lax.rem(lax.div(y, 2) + t + lax.div(t, 8), 4)
-        y2 = 2 * number + zl
-        z2 = lax.rem(z + 3 * t, 8)
-        send(
-            o_ref.at[number, z2],
-            out_ref.at[head],
-            send_sem,
-            recv_sem,
-            here,
-            (y2, x * 8 + z2, core),
-        )
+    places = [lax.rem(z + 3 * e, 8) for e in range(8)]
+    rows = out_ref.at[head]
+
+    def step(quarter, carry):
+        numbers = [lax.rem(lax.div(y, 2) + quarter + r, 4) for r in range(4)]
+        for e, z2 in enumerate(places):
+            number = numbers[e % 4]
+            piece, there = o_ref.at[number, z2], (2 * number + zl, x * 8 + z2, core)
+            if e == 0:
+                send(piece, rows, send_sem, recv_sem, here, there)
+            else:
+                remote(piece, rows, send_sem, recv_sem, there).start()
         return carry
 
-    lax.fori_loop(0, HEADS, step, 0)
+    lax.fori_loop(0, 4, step, 0)
     sent = out_ref.at[pl.ds(0, HEADS - 1)]
 
     @pl.when(same)

time: 125 us -> 126 us (level)
  the two profiles are of different devices: /device:TPU:2 before, /device:TPU:4 now
where the time goes in v3:
time: 126 us
  Pallas kernels  123 us (98%)
  local copies, waits for them, and re-layouts  1.9 us (2%)
    pallas_call x1, Pallas kernels, gather(): pl.pallas_call(functools.partial(gather_kernel, capacity), out_shape=[jax...  83.4 us
    pallas_call x1, Pallas kernels, send_back(): pl.pallas_call(return_kernel, out_shape=jax.ShapeDtypeStruct((HEADS, CHUN...  24.8 us
    pallas_call x1, Pallas kernels, attend(): pl.pallas_call(attend_kernel, out_shape=jax.ShapeDtypeStruct((GROUP_FRAME...  12.8 us

profile of v3, /device:TPU:4, one launch (start us, length us, event | category | flops | bytes accessed | tf_op | source)
XLA Modules:
  0.0 125.7 jit_solution(8178047292475105536)
XLA Ops:
  0.0 1.8 %shard_map.55 = (s32[1,512]{1,0:T(1,128)S(1)}, s32[1,256]{1,0:T(1,128)S(1)}, s32[1,128]{1,0:T(1,128)}) custom-call(s32[1,32]{1,0:T(1,128)} %bitcast.47, s32[3,160]{1,0:T(4,128)} %bitcast.46), custom_call_target="tpu_custom_call" | custom-call | tf_op jit(solution)/shard_map/pallas_call | solution.py:514
  2.5 96.4 %conditional.1 = (bf16[4,512,128]{2,1,0:T(8,128)(2,1)S(1)}) conditional(s32[]{:T(128)} %bitcast.14, (s32[512]{0:T(512)S(1)}, bf16[64,4096]{1,0:T(8,128)(2,1)}, bf16[64,4096]{1,0:T(8,128)(2,1)}, bf16[64,4096]{1,0:T(8,128)(2,1)}, s32[256]{0:T(256)S(1)}) %tuple.31, (s32[512]{0:T(512)S(1)}, bf16[64,4096]{1,0:T(8,128)(2,1)}, ...), branch_computations={%region_0.0_spmd, %region_1.0_spmd, %region_2.0_spmd, %region_3.0_... | conditional | bytes 8 | solution.py:533
  2.5 83.4 %branch_1_fun.2 = (bf16[4,8,64,128]{3,2,1,0:T(8,128)(2,1)S(1)}, bf16[13,8,64,128]{3,2,1,0:T(8,128)(2,1)S(1)}, bf16[13,8,64,128]{3,2,1,0:T(8,128)(2,1)S(1)}) custom-call(s32[512]{0:T(512)S(1)} %get-tuple-element.60.lists_ref, bf16[64,4096]{1,0:T(8,128)(2,1)} %get-tuple-element.61.q_ref, bf16[64,4096]{1,0:T(8,128)(2,1)} %get-tuple-element.62.k_ref, ...), custom_call_target="tpu_custom_call" | custom-call | tf_op jit(solution)/shard_map/cond/branch_1_fun/pallas_call | solution.py:269
  85.9 12.8 %branch_1_fun.3 = bf16[4,512,128]{2,1,0:T(8,128)(2,1)S(1)} custom-call(s32[256]{0:T(256)S(1)} %get-tuple-element.59.info_ref, bf16[4,512,128]{2,1,0:T(8,128)(2,1)S(1)} %bitcast.34, bf16[13,512,128]{2,1,0:T(8,128)(2,1)S(1)} %bitcast.29, bf16[13,512,128]{2,1,0:T(8,128)(2,1)S(1)} %bitcast.30), custom_call_target="tpu_custom_call" | custom-call | tf_op jit(solution)/shard_map/cond/branch_1_fun/pallas_call | solution.py:359
  98.9 24.8 %shard_map.56 = bf16[32,64,128]{2,1,0:T(8,128)(2,1)} custom-call(bf16[4,8,64,128]{3,2,1,0:T(8,128)(2,1)S(1)} %bitcast.37), custom_call_target="tpu_custom_call" | custom-call | tf_op jit(solution)/shard_map/pallas_call | solution.py:433
  123.8 1.9 %copy_bitcast_fusion = bf16[64,4096]{1,0:T(8,128)(2,1)} fusion(bf16[32,64,128]{2,1,0:T(8,128)(2,1)} %shard_map.56), kind=kLoop, calls=%fused_computation | loop fusion | bytes 1048576 | tf_op jit(solution)/shard_map/reshape | solution.py:441

commit v4 on v3

--- a/solution.py
+++ b/solution.py
@@ -15,7 +15,7 @@
 GROUP_FRAMES = 4
 CHUNK = 64
 SLOTS = 32
-ROOMS = (12, 13, 14, 32)
+ROOMS = (12, 13, 14, 16, 32)
 MESH = pl.DeviceIdType.MESH
 SCALE = math.log2(math.e) / math.sqrt(HEAD_DIM)
 
@@ -157,7 +157,7 @@
 
         lax.fori_loop(0, 4, step, 0)
 
-    def send_queries():
+    def send_queries(first, last):
         rows = q_out.at[lax.div(y, 2), z]
         odd = x * 8 + lax.rem(y, 2)
 
@@ -172,7 +172,7 @@
                     remote(piece, rows, send_sem.at[2], recv_sem.at[2], there).start()
             return carry
 
-        lax.fori_loop(0, 4, step, 0)
+        lax.fori_loop(first, last, step, 0)
 
     def swap(spread_ref, other_ref, number):
         for quarter in range(4):
@@ -227,9 +227,10 @@
     spread(v_ref, v_spread, 1)
     swap(k_spread, k_other, 0)
     to_mates(0, k_spread, k_stage, k_relay, k_out, 0)
-    send_queries()
+    send_queries(0, 2)
     swap(v_spread, v_other, 1)
     to_mates(0, v_spread, v_stage, v_relay, v_out, 1)
+    send_queries(2, 4)
     wait_bytes(k_other, recv_sem.at[3])
     to_mates(1, k_other, k_stage, k_relay, k_out, 0)
     pass_on(0, k_relay, k_out, 0)
@@ -308,11 +309,11 @@
             masked = jnp.where(apart[rows, near] < width, scores * SCALE, -1e30)
             high = jnp.max(masked, axis=1, keepdims=True)
             if first:
-                new_top = high
+                new_top = jnp.broadcast_to(high, (BLOCK, HEAD_DIM))
             else:
                 old_top = top[rows, :]
                 new_top = jnp.maximum(old_top, high)
-            weight = jnp.exp2(masked - new_top)
+            weight = jnp.exp2(masked - jnp.concatenate([new_top] * (near.size // HEAD_DIM), axis=1))
             product = jnp.dot(
                 weight.astype(jnp.bfloat16),
                 jnp.concatenate([v_ref[position, near, :], ones[near, :]], axis=1),
@@ -321,7 +322,8 @@
             if first:
                 weighted[rows, :] = product
             else:
-                weighted[rows, :] = weighted[rows, :] * jnp.exp2(old_top - new_top) + product
+                shrink = jnp.exp2(old_top - new_top)
+                weighted[rows, :] = weighted[rows, :] * jnp.concatenate([shrink] * 2, axis=1) + product
             top[rows, :] = new_top
 
     def one_frame(own, carry):
@@ -364,7 +366,7 @@
         scratch_shapes=[
             pltpu.VMEM((FRAME_PIX, FRAME_PIX), jnp.int32),
             pltpu.VMEM((FRAME_PIX, HEAD_DIM), jnp.bfloat16),
-            pltpu.VMEM((FRAME_PIX, 1), jnp.float32),
+            pltpu.VMEM((FRAME_PIX, HEAD_DIM), jnp.float32),
             pltpu.VMEM((FRAME_PIX, 2 * HEAD_DIM), jnp.float32),
         ],
         compiler_params=pltpu.CompilerParams(vmem_limit_bytes=40 * 2**20),

time: 126 us -> 122 us (0.968)
  the two profiles are of different devices: /device:TPU:4 before, /device:TPU:8 now
where the time goes in v4:
time: 122 us
  Pallas kernels  119 us (98%)
  local copies, waits for them, and re-layouts  1.9 us (2%)
    pallas_call x1, Pallas kernels, gather(): pl.pallas_call(functools.partial(gather_kernel, capacity), out_shape=[jax...  79.7 us
    pallas_call x1, Pallas kernels, send_back(): pl.pallas_call(return_kernel, out_shape=jax.ShapeDtypeStruct((HEADS, CHUN...  30.1 us
    pallas_call x1, Pallas kernels, attend(): pl.pallas_call(attend_kernel, out_shape=jax.ShapeDtypeStruct((GROUP_FRAME...  7.79 us

profile of v4, /device:TPU:8, one launch (start us, length us, event | category | flops | bytes accessed | tf_op | source)
XLA Modules:
  0.0 122.3 jit_solution(14343103802311280351)
XLA Ops:
  0.0 1.8 %shard_map.55 = (s32[1,512]{1,0:T(1,128)S(1)}, s32[1,256]{1,0:T(1,128)S(1)}, s32[1,128]{1,0:T(1,128)}) custom-call(s32[1,32]{1,0:T(1,128)} %bitcast.55, s32[3,160]{1,0:T(4,128)} %bitcast.54), custom_call_target="tpu_custom_call" | custom-call | tf_op jit(solution)/shard_map/pallas_call | solution.py:516
  2.5 87.8 %conditional.1 = (bf16[4,512,128]{2,1,0:T(8,128)(2,1)S(1)}) conditional(s32[]{:T(128)} %bitcast.17, (s32[512]{0:T(512)S(1)}, bf16[64,4096]{1,0:T(8,128)(2,1)}, bf16[64,4096]{1,0:T(8,128)(2,1)}, bf16[64,4096]{1,0:T(8,128)(2,1)}, s32[256]{0:T(256)S(1)}) %tuple.37, (s32[512]{0:T(512)S(1)}, bf16[64,4096]{1,0:T(8,128)(2,1)}, ...), branch_computations={%region_0.0_spmd, %region_1.0_spmd, %region_2.0_spmd, %region_3.0_... | conditional | bytes 8 | solution.py:535
  2.5 79.7 %branch_1_fun.2 = (bf16[4,8,64,128]{3,2,1,0:T(8,128)(2,1)S(1)}, bf16[13,8,64,128]{3,2,1,0:T(8,128)(2,1)S(1)}, bf16[13,8,64,128]{3,2,1,0:T(8,128)(2,1)S(1)}) custom-call(s32[512]{0:T(512)S(1)} %get-tuple-element.71.lists_ref, bf16[64,4096]{1,0:T(8,128)(2,1)} %get-tuple-element.72.q_ref, bf16[64,4096]{1,0:T(8,128)(2,1)} %get-tuple-element.73.k_ref, ...), custom_call_target="tpu_custom_call" | custom-call | tf_op jit(solution)/shard_map/cond/branch_1_fun/pallas_call | solution.py:270
  82.2 7.8 %branch_1_fun.3 = bf16[4,512,128]{2,1,0:T(8,128)(2,1)S(1)} custom-call(s32[256]{0:T(256)S(1)} %get-tuple-element.70.info_ref, bf16[4,512,128]{2,1,0:T(8,128)(2,1)S(1)} %bitcast.39, bf16[13,512,128]{2,1,0:T(8,128)(2,1)S(1)} %bitcast.34, bf16[13,512,128]{2,1,0:T(8,128)(2,1)S(1)} %bitcast.35), custom_call_target="tpu_custom_call" | custom-call | tf_op jit(solution)/shard_map/cond/branch_1_fun/pallas_call | solution.py:361
  90.3 30.1 %shard_map.56 = bf16[32,64,128]{2,1,0:T(8,128)(2,1)} custom-call(bf16[4,8,64,128]{3,2,1,0:T(8,128)(2,1)S(1)} %bitcast.43), custom_call_target="tpu_custom_call" | custom-call | tf_op jit(solution)/shard_map/pallas_call | solution.py:435
  120.3 1.9 %copy_bitcast_fusion = bf16[64,4096]{1,0:T(8,128)(2,1)} fusion(bf16[32,64,128]{2,1,0:T(8,128)(2,1)} %shard_map.56), kind=kLoop, calls=%fused_computation | loop fusion | bytes 1048576 | tf_op jit(solution)/shard_map/reshape | solution.py:443

commit v5 on v4

--- a/solution.py
+++ b/solution.py
@@ -227,10 +227,10 @@
     spread(v_ref, v_spread, 1)
     swap(k_spread, k_other, 0)
     to_mates(0, k_spread, k_stage, k_relay, k_out, 0)
-    send_queries(0, 2)
+    send_queries(0, 1)
     swap(v_spread, v_other, 1)
     to_mates(0, v_spread, v_stage, v_relay, v_out, 1)
-    send_queries(2, 4)
+    send_queries(1, 4)
     wait_bytes(k_other, recv_sem.at[3])
     to_mates(1, k_other, k_stage, k_relay, k_out, 0)
     pass_on(0, k_relay, k_out, 0)
@@ -296,10 +296,11 @@
     ones[...] = jnp.ones_like(ones)
 
     def tile(own, position, width, first, reach):
-        for block in range(FRAME_PIX // BLOCK):
-            rows = pl.ds(block * BLOCK, BLOCK)
-            low = max(0, block * BLOCK - reach)
-            near = pl.ds(low, min(FRAME_PIX, (block + 1) * BLOCK + reach) - low)
+        size = 2 * BLOCK if reach == FRAME_PIX else BLOCK
+        for block in range(FRAME_PIX // size):
+            rows = pl.ds(block * size, size)
+            low = max(0, block * size - reach)
+            near = pl.ds(low, min(FRAME_PIX, (block + 1) * size + reach) - low)
             scores = lax.dot_general(
                 q_ref[own, rows, :],
                 k_ref[position, near, :],
@@ -309,7 +310,7 @@
             masked = jnp.where(apart[rows, near] < width, scores * SCALE, -1e30)
             high = jnp.max(masked, axis=1, keepdims=True)
             if first:
-                new_top = jnp.broadcast_to(high, (BLOCK, HEAD_DIM))
+                new_top = jnp.broadcast_to(high, (size, HEAD_DIM))
             else:
                 old_top = top[rows, :]
                 new_top = jnp.maximum(old_top, high)

time: 122 us -> 122 us (level)
    pallas_call x1, Pallas kernels: 30.1 us -> 27.8 us  [send_back(): pl.pallas_call(return_kernel, out_shape=jax.ShapeDtypeStruct((HEADS, CHUN...]
    pallas_call x1, Pallas kernels: 7.79 us -> 10 us  [attend(): pl.pallas_call(attend_kernel, out_shape=jax.ShapeDtypeStruct((GROUP_FRAME...]
where the time goes in v5:
time: 122 us
  Pallas kernels  119 us (98%)
  local copies, waits for them, and re-layouts  1.9 us (2%)
    pallas_call x1, Pallas kernels, gather(): pl.pallas_call(functools.partial(gather_kernel, capacity), out_shape=[jax...  79.7 us
    pallas_call x1, Pallas kernels, send_back(): pl.pallas_call(return_kernel, out_shape=jax.ShapeDtypeStruct((HEADS, CHUN...  27.8 us
    pallas_call x1, Pallas kernels, attend(): pl.pallas_call(attend_kernel, out_shape=jax.ShapeDtypeStruct((GROUP_FRAME...  10 us

profile of v5, /device:TPU:8, one launch (start us, length us, event | category | flops | bytes accessed | tf_op | source)
XLA Modules:
  0.0 122.2 jit_solution(2252984826742152103)
XLA Ops:
  0.0 1.8 %shard_map.55 = (s32[1,512]{1,0:T(1,128)S(1)}, s32[1,256]{1,0:T(1,128)S(1)}, s32[1,128]{1,0:T(1,128)}) custom-call(s32[1,32]{1,0:T(1,128)} %bitcast.55, s32[3,160]{1,0:T(4,128)} %bitcast.54), custom_call_target="tpu_custom_call" | custom-call | tf_op jit(solution)/shard_map/pallas_call | solution.py:517
  2.5 90.0 %conditional.1 = (bf16[4,512,128]{2,1,0:T(8,128)(2,1)S(1)}) conditional(s32[]{:T(128)} %bitcast.17, (s32[512]{0:T(512)S(1)}, bf16[64,4096]{1,0:T(8,128)(2,1)}, bf16[64,4096]{1,0:T(8,128)(2,1)}, bf16[64,4096]{1,0:T(8,128)(2,1)}, s32[256]{0:T(256)S(1)}) %tuple.37, (s32[512]{0:T(512)S(1)}, bf16[64,4096]{1,0:T(8,128)(2,1)}, ...), branch_computations={%region_0.0_spmd, %region_1.0_spmd, %region_2.0_spmd, %region_3.0_... | conditional | bytes 8 | solution.py:536
  2.5 79.7 %branch_1_fun.2 = (bf16[4,8,64,128]{3,2,1,0:T(8,128)(2,1)S(1)}, bf16[13,8,64,128]{3,2,1,0:T(8,128)(2,1)S(1)}, bf16[13,8,64,128]{3,2,1,0:T(8,128)(2,1)S(1)}) custom-call(s32[512]{0:T(512)S(1)} %get-tuple-element.71.lists_ref, bf16[64,4096]{1,0:T(8,128)(2,1)} %get-tuple-element.72.q_ref, bf16[64,4096]{1,0:T(8,128)(2,1)} %get-tuple-element.73.k_ref, ...), custom_call_target="tpu_custom_call" | custom-call | tf_op jit(solution)/shard_map/cond/branch_1_fun/pallas_call | solution.py:270
  82.2 10.0 %branch_1_fun.3 = bf16[4,512,128]{2,1,0:T(8,128)(2,1)S(1)} custom-call(s32[256]{0:T(256)S(1)} %get-tuple-element.70.info_ref, bf16[4,512,128]{2,1,0:T(8,128)(2,1)S(1)} %bitcast.39, bf16[13,512,128]{2,1,0:T(8,128)(2,1)S(1)} %bitcast.34, bf16[13,512,128]{2,1,0:T(8,128)(2,1)S(1)} %bitcast.35), custom_call_target="tpu_custom_call" | custom-call | tf_op jit(solution)/shard_map/cond/branch_1_fun/pallas_call | solution.py:362
  92.5 27.8 %shard_map.56 = bf16[32,64,128]{2,1,0:T(8,128)(2,1)} custom-call(bf16[4,8,64,128]{3,2,1,0:T(8,128)(2,1)S(1)} %bitcast.43), custom_call_target="tpu_custom_call" | custom-call | tf_op jit(solution)/shard_map/pallas_call | solution.py:436
  120.3 1.9 %copy_bitcast_fusion = bf16[64,4096]{1,0:T(8,128)(2,1)} fusion(bf16[32,64,128]{2,1,0:T(8,128)(2,1)} %shard_map.56), kind=kLoop, calls=%fused_computation | loop fusion | bytes 1048576 | tf_op jit(solution)/shard_map/reshape | solution.py:444

commit v6 on v5

--- a/solution.py
+++ b/solution.py
@@ -230,9 +230,9 @@
     send_queries(0, 1)
     swap(v_spread, v_other, 1)
     to_mates(0, v_spread, v_stage, v_relay, v_out, 1)
-    send_queries(1, 4)
     wait_bytes(k_other, recv_sem.at[3])
     to_mates(1, k_other, k_stage, k_relay, k_out, 0)
+    send_queries(1, 4)
     pass_on(0, k_relay, k_out, 0)
     wait_bytes(v_other, recv_sem.at[4])
     to_mates(1, v_other, v_stage, v_relay, v_out, 1)

time: 122 us -> 122 us (level)
  the two profiles are of different devices: /device:TPU:8 before, /device:TPU:4 now
where the time goes in v6:
time: 122 us
  Pallas kernels  119 us (98%)
  local copies, waits for them, and re-layouts  1.9 us (2%)
    pallas_call x1, Pallas kernels, gather(): pl.pallas_call(functools.partial(gather_kernel, capacity), out_shape=[jax...  82.7 us
    pallas_call x1, Pallas kernels, send_back(): pl.pallas_call(return_kernel, out_shape=jax.ShapeDtypeStruct((HEADS, CHUN...  24.3 us
    pallas_call x1, Pallas kernels, attend(): pl.pallas_call(attend_kernel, out_shape=jax.ShapeDtypeStruct((GROUP_FRAME...  10.1 us

profile of v6, /device:TPU:4, one launch (start us, length us, event | category | flops | bytes accessed | tf_op | source)
XLA Modules:
  0.0 121.7 jit_solution(12021843262836504061)
XLA Ops:
  0.0 1.8 %shard_map.55 = (s32[1,512]{1,0:T(1,128)S(1)}, s32[1,256]{1,0:T(1,128)S(1)}, s32[1,128]{1,0:T(1,128)}) custom-call(s32[1,32]{1,0:T(1,128)} %bitcast.55, s32[3,160]{1,0:T(4,128)} %bitcast.54), custom_call_target="tpu_custom_call" | custom-call | tf_op jit(solution)/shard_map/pallas_call | solution.py:517
  2.5 93.0 %conditional.1 = (bf16[4,512,128]{2,1,0:T(8,128)(2,1)S(1)}) conditional(s32[]{:T(128)} %bitcast.17, (s32[512]{0:T(512)S(1)}, bf16[64,4096]{1,0:T(8,128)(2,1)}, bf16[64,4096]{1,0:T(8,128)(2,1)}, bf16[64,4096]{1,0:T(8,128)(2,1)}, s32[256]{0:T(256)S(1)}) %tuple.37, (s32[512]{0:T(512)S(1)}, bf16[64,4096]{1,0:T(8,128)(2,1)}, ...), branch_computations={%region_0.0_spmd, %region_1.0_spmd, %region_2.0_spmd, %region_3.0_... | conditional | bytes 8 | solution.py:536
  2.5 82.7 %branch_1_fun.2 = (bf16[4,8,64,128]{3,2,1,0:T(8,128)(2,1)S(1)}, bf16[13,8,64,128]{3,2,1,0:T(8,128)(2,1)S(1)}, bf16[13,8,64,128]{3,2,1,0:T(8,128)(2,1)S(1)}) custom-call(s32[512]{0:T(512)S(1)} %get-tuple-element.71.lists_ref, bf16[64,4096]{1,0:T(8,128)(2,1)} %get-tuple-element.72.q_ref, bf16[64,4096]{1,0:T(8,128)(2,1)} %get-tuple-element.73.k_ref, ...), custom_call_target="tpu_custom_call" | custom-call | tf_op jit(solution)/shard_map/cond/branch_1_fun/pallas_call | solution.py:270
  85.2 10.1 %branch_1_fun.3 = bf16[4,512,128]{2,1,0:T(8,128)(2,1)S(1)} custom-call(s32[256]{0:T(256)S(1)} %get-tuple-element.70.info_ref, bf16[4,512,128]{2,1,0:T(8,128)(2,1)S(1)} %bitcast.39, bf16[13,512,128]{2,1,0:T(8,128)(2,1)S(1)} %bitcast.34, bf16[13,512,128]{2,1,0:T(8,128)(2,1)S(1)} %bitcast.35), custom_call_target="tpu_custom_call" | custom-call | tf_op jit(solution)/shard_map/cond/branch_1_fun/pallas_call | solution.py:362
  95.5 24.3 %shard_map.56 = bf16[32,64,128]{2,1,0:T(8,128)(2,1)} custom-call(bf16[4,8,64,128]{3,2,1,0:T(8,128)(2,1)S(1)} %bitcast.43), custom_call_target="tpu_custom_call" | custom-call | tf_op jit(solution)/shard_map/pallas_call | solution.py:436
  119.8 1.9 %copy_bitcast_fusion = bf16[64,4096]{1,0:T(8,128)(2,1)} fusion(bf16[32,64,128]{2,1,0:T(8,128)(2,1)} %shard_map.56), kind=kLoop, calls=%fused_computation | loop fusion | bytes 1048576 | tf_op jit(solution)/shard_map/reshape | solution.py:444
